TPU v7x, 32 devices: a whole 2x2x4 slice. The times are simulated.
32 devices in a mesh: dp: 8 (over z, y), fsdp: 4 (over x, core).
Axes of the slice: x: 2, y: 2, z: 4, core: 2. Of those that a mesh axis runs over, the one named last changes fastest.
Arguments:
- inputs: float32 [640, 8192], P('fsdp', 'dp'), may hold values from -26 to 26, as said below
- norm_gain: float32 [640], P('fsdp'), may hold values from 0.1 to 1.9
- norm_bias: float32 [640], P('fsdp'), may hold values from -3 to 3
- conv_weight: float32 [9, 640, 640], P(None, 'fsdp'), may hold values from -0.078125 to 0.078125
- moment_one: float32 [9, 640, 640], P(None, 'fsdp'), may hold values from -3 to 3
- moment_two: float32 [9, 640, 640], P(None, 'fsdp'), may hold values from 0.5 to 4
- out_grad: float32 [640, 8192], P('fsdp', 'dp'), may hold values from -6 to 6
Outputs:
- block_out: float32 [640, 8192], P('fsdp', 'dp')
- input_grad: float32 [640, 8192], P('fsdp', 'dp')
- new_weight: float32 [9, 640, 640], P(None, 'fsdp')
- new_moment_one: float32 [9, 640, 640], P(None, 'fsdp')
- new_moment_two: float32 [9, 640, 640], P(None, 'fsdp')
Inputs may be any that keep to these rules, and one draw needn't show every extreme that they name: `inputs`: activations of mixed channel and pixel scales.
All inputs are finite; a program needn't handle non-finite values.
Results may differ from a plain program's by a relative error of at most 0.0027.
Values may be sent and summed in bfloat16 or wider, within the bound.
A program may use at most 64 MiB of HBM per device.

v0:
```python
import jax
import jax.numpy as jnp
from jax import lax
from jax.sharding import PartitionSpec as P

GROUP_CH = 40
SIDE = 32


EPS_NORM = 1e-05
BETA_ONE = 0.9
BETA_TWO = 0.999
CORRECT_ONE = 1.0 - 0.9**10
CORRECT_TWO = 1.0 - 0.999**10
LEARN_RATE = 0.001
EPS_ADAM = 1e-08
OFFSETS = ((-1, -1), (-1, 0), (-1, 1), (0, -1), (0, 0), (0, 1), (1, -1), (1, 0), (1, 1))


def shifted(source, row_step, col_step):
    width_all = source.shape[-1]
    position = jnp.arange(width_all, dtype=jnp.int32)
    row_pos = position // SIDE % SIDE
    col_pos = position % SIDE
    inside = (
        (row_pos + row_step >= 0)
        & (row_pos + row_step < SIDE)
        & (col_pos + col_step >= 0)
        & (col_pos + col_step < SIDE)
    )
    margin = SIDE + 1
    padded = jnp.pad(source, ((0, 0), (margin, margin)))
    start_at = margin + row_step * SIDE + col_step
    moved = padded[:, start_at : start_at + width_all]
    return jnp.where(inside[None, :], moved, jnp.zeros_like(moved))


def group_stats(source, norm_gain, norm_bias):
    channels, width_all = source.shape
    images = width_all // (SIDE * SIDE)
    blocks = source.reshape(channels // GROUP_CH, GROUP_CH, images, SIDE * SIDE)
    mean_val = jnp.mean(blocks, axis=(1, 3), keepdims=True)
    centred = blocks - mean_val
    var_val = jnp.mean(centred * centred, axis=(1, 3), keepdims=True)
    inv_dev = lax.rsqrt(var_val + EPS_NORM)
    normed = (centred * inv_dev).reshape(channels, width_all)
    pre_act = normed * norm_gain[:, None] + norm_bias[:, None]
    return (normed, inv_dev, pre_act)


def group_backward(grad_act, pre_act, normed, inv_dev, norm_gain):
    channels, width_all = grad_act.shape
    images = width_all // (SIDE * SIDE)
    shape_four = (channels // GROUP_CH, GROUP_CH, images, SIDE * SIDE)
    sigmoid_val = jax.nn.sigmoid(pre_act)
    grad_pre = grad_act * sigmoid_val * (1.0 + pre_act * (1.0 - sigmoid_val))
    grad_norm = (grad_pre * norm_gain[:, None]).reshape(shape_four)
    normed_four = normed.reshape(shape_four)
    mean_first = jnp.mean(grad_norm, axis=(1, 3), keepdims=True)
    mean_second = jnp.mean(grad_norm * normed_four, axis=(1, 3), keepdims=True)
    return (inv_dev * (grad_norm - mean_first - normed_four * mean_second)).reshape(
        channels, width_all
    )


def body(inputs, norm_gain, norm_bias, conv_weight, moment_one, moment_two, out_grad):
    local_ch, group_width = inputs.shape
    images = group_width // (SIDE * SIDE)
    normed, inv_dev, pre_act = group_stats(inputs, norm_gain, norm_bias)
    activation = jax.nn.silu(pre_act).astype(jnp.bfloat16)
    weight_half = conv_weight.astype(jnp.bfloat16)
    grad_half = out_grad.astype(jnp.bfloat16)
    gathered = lax.all_gather(activation, "fsdp", axis=0, tiled=True)
    conv_out = jnp.zeros((local_ch, group_width), jnp.float32)
    grad_taps = []
    for tap_index, (row_step, col_step) in enumerate(OFFSETS):
        moved = shifted(gathered, row_step, col_step)
        conv_out = conv_out + jnp.dot(
            weight_half[tap_index], moved, preferred_element_type=jnp.float32
        )
        grad_taps.append(
            lax.dot_general(
                grad_half, moved, (((1,), (1,)), ((), ())), preferred_element_type=jnp.float32
            )
        )
    block_out = inputs + conv_out
    summed = lax.psum(jnp.stack(grad_taps), "dp")
    gradient = summed / (images * lax.axis_size("dp"))
    running = jnp.zeros((local_ch * lax.axis_size("fsdp"), group_width), jnp.float32)
    for tap_index, (row_step, col_step) in enumerate(OFFSETS):
        weight_part = weight_half[tap_index]
        back_term = lax.dot_general(
            weight_part, grad_half, (((0,), (0,)), ((), ())), preferred_element_type=jnp.float32
        )
        running = running + shifted(back_term, -row_step, -col_step)
    grad_act = lax.psum_scatter(running, "fsdp", scatter_dimension=0, tiled=True)
    input_grad = out_grad + group_backward(grad_act, pre_act, normed, inv_dev, norm_gain)
    first_new = BETA_ONE * moment_one + (1.0 - BETA_ONE) * gradient
    second_new = BETA_TWO * moment_two + (1.0 - BETA_TWO) * gradient * gradient
    weight_new = conv_weight - LEARN_RATE * (first_new / CORRECT_ONE) / (
        jnp.sqrt(second_new / CORRECT_TWO) + EPS_ADAM
    )
    return (block_out, input_grad, weight_new, first_new, second_new)


def solution(mesh):
    placed = (
        P("fsdp", "dp"),
        P("fsdp"),
        P("fsdp"),
        P(None, "fsdp", None),
        P(None, "fsdp", None),
        P(None, "fsdp", None),
        P("fsdp", "dp"),
    )
    return jax.shard_map(
        body,
        mesh=mesh,
        in_specs=placed,
        out_specs=(
            P("fsdp", "dp"),
            P("fsdp", "dp"),
            P(None, "fsdp", None),
            P(None, "fsdp", None),
            P(None, "fsdp", None),
        ),
        check_vma=False,
    )
```

profile of v0, /device:TPU:0, one launch (start us, length us, event | category | flops | bytes accessed | tf_op | source)
XLA Modules:
  0.0 258.0 jit_solution(14494922928370485828)
XLA Ops:
  7.2 1.3 reduce_sum.46
  8.9 1.3 multiply_reduce_fusion.1
  10.5 2.2 multiply_convert_fusion
  13.0 20.9 %all-gather.2.cloned.1.call-done = bf16[640,1024]{1,0:T(8,128)(2,1)} async-done(((bf16[160,1024]{1,0:T(8,128)(2,1)}), bf16[640,1024]{1,0:T(8,128)(2,1)}) %all-gather.2.cloned.1.call-update) | async-done | bytes 1310736 | tf_op jit(solution)/shard_map/all_gather | solution.py:73
  33.8 2.9 %fusion.26 = f32[9,160,640]{2,1,0:T(8,128)} fusion(bf16[160,1024]{1,0:T(8,128)(2,1)S(1)} %convert_element_type.31, pred[1024]{0:T(1024)(128)(4,1)S(1)} %and_and_fusion.8, bf16[640,1024]{1,0:T(8,128)(2,1)} %all-gather.2.cloned.1.call-done), kind=kOutput, calls=%fused_computation.63 | convolution fusion | flops 210370560 | bytes 2049024 | tf_op jit(solution)/shard_map/dot_general | solution.py:82
  36.7 1.5 fusion.25
  38.2 1.5 fusion.24
  39.7 1.5 fusion.23
  41.1 1.3 fusion.22
  42.4 1.5 fusion.21
  43.9 1.5 fusion.20
  45.4 1.5 fusion.19
  46.9 1.5 fusion.18
  48.6 143.3 %all-reduce.11.cloned.1.call-done = f32[9,160,640]{2,1,0:T(8,128)} async-done(((f32[9,160,640]{2,1,0:T(8,128)}), f32[9,160,640]{2,1,0:T(8,128)}) %all-reduce.11.cloned.1.call-update) | async-done | bytes 3686416 | tf_op jit(solution)/shard_map/psum | solution.py:87
  191.9 10.9 %divide_subtract_fusion = (f32[9,160,640]{2,1,0:T(8,128)}, f32[9,160,640]{2,1,0:T(8,128)}, f32[9,160,640]{2,1,0:T(8,128)}, bf16[9,160,640]{2,1,0:T(8,128)(2,1)S(1)}) fusion(f32[9,160,640]{2,1,0:T(8,128)} %param.10, f32[9,160,640]{2,1,0:T(8,128)} %all-reduce.11.cloned.1.call-done, f32[9,160,640]{2,1,0:T(8,128)} %param.11, f32[9,160,640]{2,1,0:T(8,128)} %param.12), kind=kLoop, calls=%fused_computation | loop fusion | flops 12902400 | bytes 27648000 | tf_op jit(solution)/shard_map/sub | solution.py:100
  207.1 7.0 %fusion.8 = f32[640,1024]{1,0:T(8,128)} fusion(f32[640,1024]{1,0:T(8,128)S(1)} %fusion.46, f32[640,1024]{1,0:T(8,128)S(1)} %fusion.47, f32[640,1024]{1,0:T(8,128)S(1)} %fusion.48, f32[640,1024]{1,0:T(8,128)S(1)} %fusion.49, f32[640,1024]{1,0:T(8,128)S(1)} %fusion.50, f32[640,1024]{1,0:T(8,128)S(1)} %fusion.51, f32[640,1024]{1,0:T(8,128)S(1)} %fusion.52, ...), kind=kOutput, calls=%fused_computation.19 | convolution fusion | flops 220856320 | bytes 24134656 | tf_op jit(solution)/shard_map/dot_general | solution.py:92
  214.1 2.0 fusion.27
  216.2 0.6 convolution_add_fusion.7
  216.8 0.6 convolution_add_fusion.6
  217.5 0.6 convolution_add_fusion.5
  221.0 1.5 fusion.17
  222.5 25.5 %reduce-scatter.2.cloned.1.call-done = f32[160,1024]{1,0:T(8,128)} async-done(((f32[640,1024]{1,0:T(8,128)}), f32[160,1024]{1,0:T(8,128)}) %reduce-scatter.2.cloned.1.call-update) | async-done | bytes 655376 | tf_op jit(solution)/shard_map/reduce_scatter | solution.py:96
  248.0 1.6 fusion.104
  250.4 1.1 multiply_add_fusion.2
  (56 shorter events, 9.1 us)
Async XLA Ops:
  7.2 5.7 %copy-start.1 = (f32[160,1024]{1,0:T(8,128)S(1)}, f32[160,1024]{1,0:T(8,128)}, u32[]{:S(2)}) copy-start(f32[160,1024]{1,0:T(8,128)} %param.13) | copy-start | bytes 1966084
  7.2 26.7 %all-gather.2.cloned.1.call-start = ((), (), s32[]{:S(2)}) async-start(), calls=%async_computation.1 | async-start | bytes 1638400 | tf_op jit(solution)/shard_map/all_gather | solution.py:73
  12.8 179.1 %all-reduce.11.cloned.1.call-start = ((), (), s32[]{:S(2)}) async-start(), calls=%async_computation.3 | async-start | bytes 7372800 | tf_op jit(solution)/shard_map/psum | solution.py:87
  33.8 2.9 %copy-start.4 = (bf16[640,1024]{1,0:T(8,128)(2,1)S(1)}, bf16[640,1024]{1,0:T(8,128)(2,1)}, u32[]{:S(2)}) copy-start(bf16[640,1024]{1,0:T(8,128)(2,1)} %all-gather.2.cloned.1.call-done) | copy-start | bytes 3932164
  48.3 199.6 %reduce-scatter.2.cloned.1.call-start = ((), (), s32[]{:S(2)}) async-start(), calls=%async_computation.2 | async-start | bytes 3276800 | tf_op jit(solution)/shard_map/reduce_scatter | solution.py:96
  214.1 2.1 copy-start.5
  219.8 1.2 copy-start
  221.0 26.9 %copy-start.2 = (f32[160]{0:T(256)S(1)}, f32[160]{0:T(256)}, u32[]{:S(2)}) copy-start(f32[160]{0:T(256)} %param.9) | copy-start | bytes 1924
  221.0 26.9 %copy-start.3 = (f32[160]{0:T(256)S(1)}, f32[160]{0:T(256)}, u32[]{:S(2)}) copy-start(f32[160]{0:T(256)} %param.8) | copy-start | bytes 1924
Sparse Core Ops, SparseCore 0:
  12.9 20.8 all-gather.1
  48.5 143.3 all-reduce.10
  214.2 33.6 reduce-scatter.1
where the time goes:
time: 258 us
  waiting for transfers between devices  190 us (74%)
  matrix products  33.6 us (13%)
  other arithmetic  19 us (7%)
  between operations  13.9 us (5%)
    psum x1, waiting for transfers between devices, body(): summed = lax.psum(jnp.stack(grad_taps), 'dp')  143 us
    reduce_scatter x1, waiting for transfers between devices, body(): lax.psum_scatter(running, 'fsdp', scatter_dimension=0, tiled=True)  25.5 us
    all_gather x1, waiting for transfers between devices, body(): gathered = lax.all_gather(activation, 'fsdp', axis=0, tiled=True)  20.9 us
    dot_general x9, matrix products, body(): lax.dot_general(grad_half, moved, (((1,), (1,)), ((), ())), preferred_ele...  14.5 us
    dot_general x9, matrix products, body(): lax.dot_general(weight_part, grad_half, (((0,), (0,)), ((), ())), preferr...  11.3 us
    sub x1, other arithmetic, body(): conv_weight - LEARN_RATE * (first_new / CORRECT_ONE) / (jnp.sqrt(second_n...  10.9 us
    dot_general x9, matrix products, body(): jnp.dot(weight_half[tap_index], moved, preferred_element_type=jnp.float32)  7.75 us
  transfers between devices with their start and end apart: 3, of which 3 were waited for; matrix products, arithmetic and copies ran while one was open for 3% of the time, Pallas kernels for 0%

commit v1 on v0

--- a/solution.py
+++ b/solution.py
@@ -1,6 +1,10 @@
+import functools
+
 import jax
 import jax.numpy as jnp
 from jax import lax
+from jax.experimental import pallas as pl
+from jax.experimental.pallas import tpu as pltpu
 from jax.sharding import PartitionSpec as P
 
 GROUP_CH = 40
@@ -103,6 +107,403 @@
     return (block_out, input_grad, weight_new, first_new, second_new)
 
 
+CHUNKS = 6
+VMEM_STEP = 36 * 1024 * 1024
+DP_Y = 2
+DP_Z = 4
+FSDP = 4
+MESH = pl.DeviceIdType.MESH
+
+
+def tap_mask(row_step, col_step):
+    position = lax.broadcasted_iota(jnp.int32, (1, SIDE * SIDE), 1)
+    row_pos = position // SIDE + row_step
+    col_pos = position % SIDE + col_step
+    inside = (row_pos >= 0) & (row_pos < SIDE) & (col_pos >= 0) & (col_pos < SIDE)
+    return inside
+
+
+def lane_shift(value, row_step, col_step):
+    step = row_step * SIDE + col_step
+    if step == 0:
+        return value
+    moved = pltpu.roll(value, (-step) % (SIDE * SIDE), 1)
+    return jnp.where(tap_mask(row_step, col_step), moved, 0.0)
+
+
+def step_kernel(
+    x_ref,
+    gain_ref,
+    bias_ref,
+    w_ref,
+    g_ref,
+    block_ref,
+    igrad_ref,
+    out_ref,
+    w_full,
+    w_half,
+    act,
+    shifted_g,
+    normed_ref,
+    pre_ref,
+    back,
+    from_sib,
+    to_x,
+    from_x,
+    own_full,
+    part,
+    from_y,
+    half_full,
+    half_sum,
+    from_z,
+    w_sem,
+    send_sem,
+    recv_sem,
+):
+    local_ch, width = x_ref.shape
+    taps = len(OFFSETS)
+    all_rows = part.shape[0]
+    chunk = all_rows // CHUNKS
+    half = chunk // DP_Y
+    shard = half // DP_Z
+    dp, fs = lax.axis_index("dp"), lax.axis_index("fsdp")
+    pos_z, pos_y = dp // DP_Y, dp % DP_Y
+    sib = fs // 2 * 2 + (1 - fs % 2)
+    far = (fs + 2) % FSDP
+    far_sib = (sib + 2) % FSDP
+    sib_id, far_id = (dp, sib), (dp, far)
+    y_id = (pos_z * DP_Y + (1 - pos_y), fs)
+    z_ids = [((pos_z + d) % DP_Z * DP_Y + pos_y, fs) for d in range(1, DP_Z)]
+    next_z = pos_z // 2 * 2 + (1 - pos_z % 2)
+    next_id, skip_id = (next_z * DP_Y + pos_y, fs), z_ids[1]
+
+    w_copy = pltpu.make_async_copy(w_ref, w_full, w_sem)
+    w_copy.start()
+    barrier = pltpu.get_barrier_semaphore()
+    peers = [sib_id, far_id, y_id] + z_ids
+    for peer in peers:
+        pl.semaphore_signal(barrier, inc=1, device_id=peer, device_id_type=MESH)
+
+    def rows_of(index):
+        return pl.ds(pl.multiple_of(index * local_ch, local_ch), local_ch)
+
+    def remote(source, target, index, peer):
+        return pltpu.make_async_remote_copy(
+            src_ref=source,
+            dst_ref=target,
+            send_sem=send_sem.at[index],
+            recv_sem=recv_sem.at[index],
+            device_id=peer,
+            device_id_type=MESH,
+        )
+
+    mine = rows_of(fs)
+    inv_devs = []
+    count = 1.0 / (GROUP_CH * width)
+    pieces = []
+    for group in range(local_ch // GROUP_CH):
+        rows = slice(group * GROUP_CH, (group + 1) * GROUP_CH)
+        value = x_ref[rows, :]
+        mean_val = jnp.sum(value) * count
+        centred = value - mean_val
+        var_val = jnp.sum(centred * centred) * count
+        inv_dev = lax.rsqrt(jnp.full((1, 1), var_val + EPS_NORM, jnp.float32))
+        inv_devs.append(inv_dev)
+        normed = centred * inv_dev
+        pre_act = normed * gain_ref[rows, :] + bias_ref[rows, :]
+        normed_ref[rows, :] = normed
+        pre_ref[rows, :] = pre_act
+        pieces.append(pre_act * jax.nn.sigmoid(pre_act))
+    act[mine, :] = jnp.concatenate(pieces, axis=0).astype(jnp.bfloat16)
+
+    pl.semaphore_wait(barrier, len(peers))
+    act_sib = remote(act.at[mine], act.at[mine], 0, sib_id)
+    act_far = remote(act.at[mine], act.at[mine], 1, far_id)
+    act_far.start()
+    act_sib.start()
+
+    for tap, (row_step, col_step) in enumerate(OFFSETS):
+        shifted_g[tap * local_ch : (tap + 1) * local_ch, :] = lane_shift(
+            g_ref[...], -row_step, -col_step
+        ).astype(jnp.bfloat16)
+    spare = all_rows - taps * local_ch
+    shifted_g[taps * local_ch :, :] = jnp.zeros((spare, width), jnp.bfloat16)
+
+    w_copy.wait()
+    w_half[...] = w_full[...].astype(jnp.bfloat16)
+
+    tile = 512
+
+    def back_tile(step, carry):
+        columns = pl.ds(pl.multiple_of(step * tile, tile), tile)
+        back[:, columns] = lax.dot_general(
+            w_half[...],
+            shifted_g[: taps * local_ch, columns],
+            (((0,), (0,)), ((), ())),
+            preferred_element_type=jnp.float32,
+        ).astype(jnp.bfloat16)
+        return carry
+
+    lax.fori_loop(0, width // tile, back_tile, 0)
+    back_far = remote(back.at[rows_of(far_sib)], from_sib.at[1], 4, sib_id)
+    back_own = remote(back.at[rows_of(sib)], from_sib.at[0], 3, sib_id)
+    back_far.start()
+    back_own.start()
+
+    act_far.wait_recv()
+    act_forward = remote(act.at[rows_of(far)], act.at[rows_of(far)], 2, sib_id)
+    act_forward.start()
+    act_sib.wait_recv()
+    act_forward.wait_recv()
+
+    y_copies, z_copies, skip_copies, next_copies, yg_copies = [], [], [], [], []
+
+    def half_rows(step, index):
+        return pl.ds(pl.multiple_of(step * chunk + index * half, half), half)
+
+    def partial_sum(step):
+        rows = slice(step * chunk, (step + 1) * chunk)
+        product = lax.dot_general(
+            shifted_g[rows, :],
+            act[...],
+            (((1,), (1,)), ((), ())),
+            preferred_element_type=jnp.float32,
+        )
+        own_full[rows, :] = product
+        part[rows, :] = product.astype(jnp.bfloat16)
+        copy = remote(part.at[half_rows(step, 1 - pos_y)], from_y.at[step], 6 + 8 * step, y_id)
+        copy.start()
+        y_copies.append(copy)
+
+    def place(index_z):
+        return index_z % 2 * 2 + index_z // 2
+
+    def shard_rows(index_z):
+        return pl.ds(pl.multiple_of(place(index_z) * shard, shard), shard)
+
+    def sum_pair(step):
+        y_copies[step].wait_recv()
+        total = own_full[half_rows(step, pos_y), :] + from_y[step].astype(jnp.float32)
+        half_full[step] = total
+        half_sum[step] = total.astype(jnp.bfloat16)
+        copies = []
+        for d in (2, 1, 3):
+            copy = remote(
+                half_sum.at[step, shard_rows((pos_z + d) % DP_Z)],
+                from_z.at[step, d - 1],
+                6 + 8 * step + d,
+                z_ids[d - 1],
+            )
+            copy.start()
+            copies.append(copy)
+        z_copies.append(copies)
+
+    def sum_line(step):
+        for copy in z_copies[step]:
+            copy.wait_recv()
+        total = half_full[step, shard_rows(pos_z), :]
+        for d in range(DP_Z - 1):
+            total = total + from_z[step, d].astype(jnp.float32)
+        start = step * chunk + pos_y * half + place(pos_z) * shard
+        rows = pl.ds(pl.multiple_of(start, shard), shard)
+        out_ref[rows, :] = total.astype(jnp.bfloat16)
+        copy = remote(out_ref.at[rows], out_ref.at[rows], 6 + 8 * step + 4, skip_id)
+        copy.start()
+        skip_copies.append(copy)
+
+    def share_pair(step):
+        skip_copies[step].wait_recv()
+        start = step * chunk + pos_y * half + pos_z % 2 * 2 * shard
+        rows = pl.ds(pl.multiple_of(start, 2 * shard), 2 * shard)
+        copy = remote(out_ref.at[rows], out_ref.at[rows], 6 + 8 * step + 5, next_id)
+        copy.start()
+        next_copies.append(copy)
+
+    def share_half(step):
+        next_copies[step].wait_recv()
+        rows = half_rows(step, pos_y)
+        copy = remote(out_ref.at[rows], out_ref.at[rows], 6 + 8 * step + 7, y_id)
+        copy.start()
+        yg_copies.append(copy)
+
+    def conv_taps(first, last):
+        total = x_ref[...] if first == 0 else block_ref[...]
+        for tap in range(first, last):
+            product = jnp.dot(
+                w_half[tap * local_ch : (tap + 1) * local_ch, :],
+                act[...],
+                preferred_element_type=jnp.float32,
+            )
+            total = total + lane_shift(product, *OFFSETS[tap])
+        block_ref[...] = total
+
+    partial_sum(0)
+    partial_sum(1)
+    back_far.wait_recv()
+    to_x[...] = (
+        back[rows_of(far), :].astype(jnp.float32) + from_sib[1].astype(jnp.float32)
+    ).astype(jnp.bfloat16)
+    back_x = remote(to_x, from_x, 5, far_id)
+    back_x.start()
+    partial_sum(2)
+    sum_pair(0)
+    partial_sum(3)
+    partial_sum(4)
+    sum_pair(1)
+    partial_sum(5)
+    conv_taps(0, 3)
+    sum_line(0)
+    sum_pair(2)
+    conv_taps(3, 6)
+    share_pair(0)
+    sum_line(1)
+    sum_pair(3)
+    conv_taps(6, 9)
+    share_half(0)
+    share_pair(1)
+    sum_line(2)
+    sum_pair(4)
+
+    back_own.wait_recv()
+    back_x.wait_recv()
+    for group in range(local_ch // GROUP_CH):
+        rows = slice(group * GROUP_CH, (group + 1) * GROUP_CH)
+        grad_act = (
+            back[mine, :].astype(jnp.float32)[rows]
+            + from_sib[0].astype(jnp.float32)[rows]
+            + from_x[...].astype(jnp.float32)[rows]
+        )
+        pre_act, normed = pre_ref[rows, :], normed_ref[rows, :]
+        sigmoid_val = jax.nn.sigmoid(pre_act)
+        grad_pre = grad_act * sigmoid_val * (1.0 + pre_act * (1.0 - sigmoid_val))
+        grad_norm = grad_pre * gain_ref[rows, :]
+        mean_first = jnp.sum(grad_norm) * count
+        mean_second = jnp.sum(grad_norm * normed) * count
+        igrad_ref[rows, :] = g_ref[rows, :] + inv_devs[group] * (
+            grad_norm - mean_first - normed * mean_second
+        )
+
+    share_half(1)
+    share_pair(2)
+    sum_line(3)
+    sum_pair(5)
+    share_half(2)
+    share_pair(3)
+    sum_line(4)
+    share_half(3)
+    share_pair(4)
+    sum_line(5)
+    share_half(4)
+    share_pair(5)
+    share_half(5)
+    for copy in yg_copies:
+        copy.wait_recv()
+    for copy in [act_sib, act_far, act_forward, back_far, back_own, back_x]:
+        copy.wait_send()
+    for copies in z_copies + [skip_copies, next_copies, y_copies, yg_copies]:
+        for copy in copies:
+            copy.wait_send()
+
+
+def adam_kernel(scale, sum_ref, w_ref, one_ref, two_ref, w_out, one_out, two_out):
+    gradient = sum_ref[...].astype(jnp.float32) * scale
+    first_new = BETA_ONE * one_ref[...] + (1.0 - BETA_ONE) * gradient
+    second_new = BETA_TWO * two_ref[...] + (1.0 - BETA_TWO) * gradient * gradient
+    one_out[...] = first_new
+    two_out[...] = second_new
+    w_out[...] = w_ref[...] - LEARN_RATE * (first_new / CORRECT_ONE) / (
+        jnp.sqrt(second_new / CORRECT_TWO) + EPS_ADAM
+    )
+
+
+def fused_body(inputs, norm_gain, norm_bias, conv_weight, moment_one, moment_two, out_grad):
+    local_ch, width = inputs.shape
+    taps, _, channels = conv_weight.shape
+    unit = 16 * DP_Y * DP_Z * CHUNKS
+    all_rows = (taps * local_ch + unit - 1) // unit * unit
+    half = all_rows // CHUNKS // DP_Y
+    shard = half // DP_Z
+    copies = 6 + 8 * CHUNKS
+    vmem = pl.BlockSpec(memory_space=pltpu.VMEM)
+    flops = 2 * 3 * taps * local_ch * channels * width
+    block_out, input_grad, summed = pl.pallas_call(
+        step_kernel,
+        out_shape=(
+            jax.ShapeDtypeStruct(inputs.shape, jnp.float32),
+            jax.ShapeDtypeStruct(inputs.shape, jnp.float32),
+            jax.ShapeDtypeStruct((all_rows, channels), jnp.bfloat16),
+        ),
+        in_specs=[vmem, vmem, vmem, pl.BlockSpec(memory_space=pl.ANY), vmem],
+        out_specs=(vmem, vmem, vmem),
+        scratch_shapes=[
+            pltpu.VMEM((taps * local_ch, channels), jnp.float32),
+            pltpu.VMEM((taps * local_ch, channels), jnp.bfloat16),
+            pltpu.VMEM((channels, width), jnp.bfloat16),
+            pltpu.VMEM((all_rows, width), jnp.bfloat16),
+            pltpu.VMEM((local_ch, width), jnp.float32),
+            pltpu.VMEM((local_ch, width), jnp.float32),
+            pltpu.VMEM((channels, width), jnp.bfloat16),
+            pltpu.VMEM((2, local_ch, width), jnp.bfloat16),
+            pltpu.VMEM((local_ch, width), jnp.bfloat16),
+            pltpu.VMEM((local_ch, width), jnp.bfloat16),
+            pltpu.VMEM((all_rows, channels), jnp.float32),
+            pltpu.VMEM((all_rows, channels), jnp.bfloat16),
+            pltpu.VMEM((CHUNKS, half, channels), jnp.bfloat16),
+            pltpu.VMEM((CHUNKS, half, channels), jnp.float32),
+            pltpu.VMEM((CHUNKS, half, channels), jnp.bfloat16),
+            pltpu.VMEM((CHUNKS, DP_Z - 1, shard, channels), jnp.bfloat16),
+            pltpu.SemaphoreType.DMA,
+            pltpu.SemaphoreType.DMA((copies,)),
+            pltpu.SemaphoreType.DMA((copies,)),
+        ],
+        compiler_params=pltpu.CompilerParams(
+            collective_id=0, has_side_effects=True, vmem_limit_bytes=VMEM_STEP
+        ),
+        cost_estimate=pl.CostEstimate(
+            flops=flops, bytes_accessed=8_000_000, transcendentals=4 * local_ch * width
+        ),
+    )(
+        inputs,
+        norm_gain[:, None],
+        norm_bias[:, None],
+        conv_weight.reshape(taps * local_ch, channels),
+        out_grad,
+    )
+    flat = (taps * local_ch, channels)
+    scale = 1.0 / (lax.axis_size("dp") * (width // (SIDE * SIDE)))
+    block = pl.BlockSpec((local_ch, channels), lambda step: (step, 0))
+    updated = pl.pallas_call(
+        functools.partial(adam_kernel, scale),
+        grid=(taps,),
+        out_shape=(jax.ShapeDtypeStruct(flat, jnp.float32),) * 3,
+        in_specs=[block] * 4,
+        out_specs=(block,) * 3,
+        cost_estimate=pl.CostEstimate(
+            flops=16 * flat[0] * flat[1],
+            bytes_accessed=26 * flat[0] * flat[1],
+            transcendentals=2 * flat[0] * flat[1],
+        ),
+        compiler_params=pltpu.CompilerParams(vmem_limit_bytes=16 * 1024 * 1024),
+    )(
+        summed,
+        conv_weight.reshape(flat),
+        moment_one.reshape(flat),
+        moment_two.reshape(flat),
+    )
+    weight_new, first_new, second_new = [leaf.reshape(conv_weight.shape) for leaf in updated]
+    return (block_out, input_grad, weight_new, first_new, second_new)
+
+
+def pick_body(inputs, *rest):
+    fits = (
+        lax.axis_size("dp") == DP_Y * DP_Z
+        and lax.axis_size("fsdp") == FSDP
+        and inputs.shape[1] == SIDE * SIDE
+        and inputs.shape[0] % 16 == 0
+    )
+    return (fused_body if fits else body)(inputs, *rest)
+
+
 def solution(mesh):
     placed = (
         P("fsdp", "dp"),
@@ -114,7 +515,7 @@
         P("fsdp", "dp"),
     )
     return jax.shard_map(
-        body,
+        pick_body,
         mesh=mesh,
         in_specs=placed,
         out_specs=(

time: 258 us -> 82 us (0.32)
  waiting for transfers between devices: 190 us -> 0 us
  Pallas kernels: 0 us -> 73.6 us
  matrix products: 33.6 us -> 0 us
  other arithmetic: 19 us -> 0 us
  between operations: 13.9 us -> 0.68 us
  local copies, waits for them, and re-layouts: 1.53 us -> 7.46 us
    psum x1 -> x0, waiting for transfers between devices: 143 us -> none  [body(): summed = lax.psum(jnp.stack(grad_taps), 'dp')]
    pallas_call x0 -> x2, Pallas kernels: none -> 73.6 us  [the longest x1 67.4 us: fused_body(): pl.pallas_call(step_kernel, out_shape=(jax.ShapeDtypeStruct(inputs.shape,...]
    dot_general x27 -> x0, matrix products: 33.6 us -> none  [the longest x9 14.5 us: body(): lax.dot_general(grad_half, moved, (((1,), (1,)), ((), ())), preferred_ele...]
    reduce_scatter x1 -> x0, waiting for transfers between devices: 25.5 us -> none  [body(): lax.psum_scatter(running, 'fsdp', scatter_dimension=0, tiled=True)]
    all_gather x1 -> x0, waiting for transfers between devices: 20.9 us -> none  [body(): gathered = lax.all_gather(activation, 'fsdp', axis=0, tiled=True)]
    sub x1 -> x0, other arithmetic: 10.9 us -> none  [body(): conv_weight - LEARN_RATE * (first_new / CORRECT_ONE) / (jnp.sqrt(second_n...]
    unnamed x12, local copies, waits for them, and re-layouts: 0.57 us -> 5.89 us
    reduce_sum x7 -> x0, other arithmetic: 4.7 us -> none  [the longest x2 1.76 us: group_backward(): mean_first = jnp.mean(grad_norm, axis=(1, 3), keepdims=True)]
  transfers between devices with their start and end apart: 3 -> 0, of which waited for: 3 -> 0; matrix products, arithmetic and copies ran while one was open for 3% -> 0% of each run, Pallas kernels for 0% -> 0%
where the time goes in v1:
time: 82 us; the launch traced here: 81.8 us
  Pallas kernels  73.6 us (90%)
  local copies, waits for them, and re-layouts  7.46 us (9%)
    pallas_call x1, Pallas kernels, fused_body(): pl.pallas_call(step_kernel, out_shape=(jax.ShapeDtypeStruct(inputs.shape,...  67.4 us
    pallas_call x1, Pallas kernels, fused_body(): pl.pallas_call(functools.partial(adam_kernel, scale), grid=(taps,), out_s...  6.2 us
    unnamed x12, local copies, waits for them, and re-layouts  5.89 us

profile of v1, /device:TPU:0, one launch (start us, length us, event | category | flops | bytes accessed | tf_op | source)
XLA Modules:
  0.0 81.8 jit_solution(14365292571370640371)
XLA Ops:
  0.6 0.8 copy.12.gain_ref
  1.4 0.8 copy.13.bias_ref
  2.2 0.0 copy-start
  2.2 2.0 %copy-done = f32[9,160,640]{2,1,0:T(8,128)S(1)} copy-done((f32[9,160,640]{2,1,0:T(8,128)S(1)}, f32[9,160,640]{2,1,0:T(8,128)}, u32[]{:S(2)}) %copy-start) | copy-done | bytes 3686424
  4.3 0.0 copy-start.3
  4.3 1.1 %copy-done.3 = f32[160,1024]{1,0:T(8,128)S(1)} copy-done((f32[160,1024]{1,0:T(8,128)S(1)}, f32[160,1024]{1,0:T(8,128)}, u32[]{:S(2)}) %copy-start.3) | copy-done | bytes 655384
  5.3 0.0 copy-start.4
  5.4 1.1 %copy-done.4 = f32[160,1024]{1,0:T(8,128)S(1)} copy-done((f32[160,1024]{1,0:T(8,128)S(1)}, f32[160,1024]{1,0:T(8,128)}, u32[]{:S(2)}) %copy-start.4) | copy-done | bytes 655384
  6.4 0.0 copy-start.1
  6.4 0.0 copy-start.2
  6.4 67.4 %shard_map.110 = (f32[160,1024]{1,0:T(8,128)S(1)}, f32[160,1024]{1,0:T(8,128)S(1)}, bf16[1536,640]{1,0:T(8,128)(2,1)S(1)}) custom-call(f32[160,1024]{1,0:T(8,128)S(1)} %copy-done.3, f32[160,1]{1,0:T(8,128)S(1)} %copy.12.gain_ref, f32[160,1]{1,0:T(8,128)S(1)} %copy.13.bias_ref, f32[1440,640]{1,0:T(8,128)S(1)} %bitcast.8, f32[160,1024]{1,0:T(8,128)S(1)} %copy-done.4), custom_call_target="tpu_custom_call" | custom-call | flops 5662310400 | bytes 8000000 | tf_op jit(solution)/shard_map/pallas_call | solution.py:429
  73.9 0.0 copy-done.1
  73.9 0.0 copy-done.2
  73.9 6.2 %shard_map.111 = (f32[1440,640]{1,0:T(8,128)}, f32[1440,640]{1,0:T(8,128)}, f32[1440,640]{1,0:T(8,128)}) custom-call(bf16[1536,640]{1,0:T(8,128)(2,1)S(1)} %get-tuple-element.13.sum_ref, f32[1440,640]{1,0:T(8,128)S(1)} %bitcast.9, f32[1440,640]{1,0:T(8,128)S(1)} %bitcast.10, f32[1440,640]{1,0:T(8,128)S(1)} %bitcast.11), custom_call_target="tpu_custom_call" | custom-call | flops 14745600 | bytes 23961600 | tf_op jit(solution)/shard_map/pallas_call | solution.py:475
  80.1 0.8 %copy.16 = f32[160,1024]{1,0:T(8,128)} copy(f32[160,1024]{1,0:T(8,128)S(1)} %get-tuple-element.22) | data formatting | bytes 1310720
  80.9 0.8 %copy.17 = f32[160,1024]{1,0:T(8,128)} copy(f32[160,1024]{1,0:T(8,128)S(1)} %get-tuple-element.23) | data formatting | bytes 1310720
Async XLA Ops:
  2.2 2.0 %copy-start = (f32[9,160,640]{2,1,0:T(8,128)S(1)}, f32[9,160,640]{2,1,0:T(8,128)}, u32[]{:S(2)}) copy-start(f32[9,160,640]{2,1,0:T(8,128)} %param.10) | copy-start | bytes 11059204
  4.3 1.1 %copy-start.3 = (f32[160,1024]{1,0:T(8,128)S(1)}, f32[160,1024]{1,0:T(8,128)}, u32[]{:S(2)}) copy-start(f32[160,1024]{1,0:T(8,128)} %x_ref.1) | copy-start | bytes 1966084
  5.3 1.1 %copy-start.4 = (f32[160,1024]{1,0:T(8,128)S(1)}, f32[160,1024]{1,0:T(8,128)}, u32[]{:S(2)}) copy-start(f32[160,1024]{1,0:T(8,128)} %g_ref.1) | copy-start | bytes 1966084
  6.4 67.4 %copy-start.1 = (f32[9,160,640]{2,1,0:T(8,128)S(1)}, f32[9,160,640]{2,1,0:T(8,128)}, u32[]{:S(2)}) copy-start(f32[9,160,640]{2,1,0:T(8,128)} %param.11) | copy-start | bytes 11059204
  6.4 67.4 %copy-start.2 = (f32[9,160,640]{2,1,0:T(8,128)S(1)}, f32[9,160,640]{2,1,0:T(8,128)}, u32[]{:S(2)}) copy-start(f32[9,160,640]{2,1,0:T(8,128)} %param.12) | copy-start | bytes 11059204

commit v2 on v1

--- a/solution.py
+++ b/solution.py
@@ -132,37 +132,39 @@
 
 
 def step_kernel(
-    x_ref,
-    gain_ref,
-    bias_ref,
+    x_hbm,
+    affine_ref,
     w_ref,
-    g_ref,
+    g_hbm,
     block_ref,
     igrad_ref,
     out_ref,
+    x_ref,
+    g_ref,
     w_full,
     w_half,
     act,
+    act_next,
+    g_half,
+    g_next,
     shifted_g,
+    shifted_next,
     normed_ref,
     pre_ref,
     back,
     from_sib,
     to_x,
     from_x,
-    own_full,
-    part,
-    from_y,
     half_full,
     half_sum,
     from_z,
-    w_sem,
+    load_sem,
     send_sem,
     recv_sem,
 ):
     local_ch, width = x_ref.shape
     taps = len(OFFSETS)
-    all_rows = part.shape[0]
+    all_rows = shifted_g.shape[0]
     chunk = all_rows // CHUNKS
     half = chunk // DP_Y
     shard = half // DP_Z
@@ -177,7 +179,11 @@
     next_z = pos_z // 2 * 2 + (1 - pos_z % 2)
     next_id, skip_id = (next_z * DP_Y + pos_y, fs), z_ids[1]
 
-    w_copy = pltpu.make_async_copy(w_ref, w_full, w_sem)
+    x_copy = pltpu.make_async_copy(x_hbm, x_ref, load_sem.at[0])
+    g_copy = pltpu.make_async_copy(g_hbm, g_ref, load_sem.at[1])
+    w_copy = pltpu.make_async_copy(w_ref, w_full, load_sem.at[2])
+    x_copy.start()
+    g_copy.start()
     w_copy.start()
     barrier = pltpu.get_barrier_semaphore()
     peers = [sib_id, far_id, y_id] + z_ids
@@ -201,6 +207,7 @@
     inv_devs = []
     count = 1.0 / (GROUP_CH * width)
     pieces = []
+    x_copy.wait()
     for group in range(local_ch // GROUP_CH):
         rows = slice(group * GROUP_CH, (group + 1) * GROUP_CH)
         value = x_ref[rows, :]
@@ -210,7 +217,7 @@
         inv_dev = lax.rsqrt(jnp.full((1, 1), var_val + EPS_NORM, jnp.float32))
         inv_devs.append(inv_dev)
         normed = centred * inv_dev
-        pre_act = normed * gain_ref[rows, :] + bias_ref[rows, :]
+        pre_act = normed * affine_ref[rows, 0:1] + affine_ref[rows, 1:2]
         normed_ref[rows, :] = normed
         pre_ref[rows, :] = pre_act
         pieces.append(pre_act * jax.nn.sigmoid(pre_act))
@@ -219,8 +226,15 @@
     pl.semaphore_wait(barrier, len(peers))
     act_sib = remote(act.at[mine], act.at[mine], 0, sib_id)
     act_far = remote(act.at[mine], act.at[mine], 1, far_id)
+    extra = 6 + 8 * CHUNKS
+    act_y = remote(act.at[mine], act_next.at[mine], extra, y_id)
+    act_y.start()
     act_far.start()
     act_sib.start()
+    g_copy.wait()
+    g_half[...] = g_ref[...].astype(jnp.bfloat16)
+    g_y = remote(g_half, g_next, extra + 1, y_id)
+    g_y.start()
 
     for tap, (row_step, col_step) in enumerate(OFFSETS):
         shifted_g[tap * local_ch : (tap + 1) * local_ch, :] = lane_shift(
@@ -228,6 +242,7 @@
         ).astype(jnp.bfloat16)
     spare = all_rows - taps * local_ch
     shifted_g[taps * local_ch :, :] = jnp.zeros((spare, width), jnp.bfloat16)
+    shifted_next[taps * local_ch :, :] = jnp.zeros((spare, width), jnp.bfloat16)
 
     w_copy.wait()
     w_half[...] = w_full[...].astype(jnp.bfloat16)
@@ -250,30 +265,31 @@
     back_far.start()
     back_own.start()
 
+    act_y.wait_recv()
+    next_far = remote(act_next.at[mine], act_next.at[mine], extra + 2, far_id)
+    next_sib = remote(act_next.at[mine], act_next.at[mine], extra + 3, sib_id)
+    next_far.start()
+    next_sib.start()
     act_far.wait_recv()
     act_forward = remote(act.at[rows_of(far)], act.at[rows_of(far)], 2, sib_id)
     act_forward.start()
     act_sib.wait_recv()
-    act_forward.wait_recv()
-
-    y_copies, z_copies, skip_copies, next_copies, yg_copies = [], [], [], [], []
+
+    z_copies, skip_copies, next_copies, yg_copies = [], [], [], []
 
     def half_rows(step, index):
         return pl.ds(pl.multiple_of(step * chunk + index * half, half), half)
 
-    def partial_sum(step):
-        rows = slice(step * chunk, (step + 1) * chunk)
-        product = lax.dot_general(
-            shifted_g[rows, :],
-            act[...],
+    def product(left, right, step):
+        return lax.dot_general(
+            left[half_rows(step, pos_y), :],
+            right[...],
             (((1,), (1,)), ((), ())),
             preferred_element_type=jnp.float32,
         )
-        own_full[rows, :] = product
-        part[rows, :] = product.astype(jnp.bfloat16)
-        copy = remote(part.at[half_rows(step, 1 - pos_y)], from_y.at[step], 6 + 8 * step, y_id)
-        copy.start()
-        y_copies.append(copy)
+
+    def own_sum(step):
+        half_full[step] = product(shifted_g, act, step)
 
     def place(index_z):
         return index_z % 2 * 2 + index_z // 2
@@ -282,8 +298,7 @@
         return pl.ds(pl.multiple_of(place(index_z) * shard, shard), shard)
 
     def sum_pair(step):
-        y_copies[step].wait_recv()
-        total = own_full[half_rows(step, pos_y), :] + from_y[step].astype(jnp.float32)
+        total = half_full[step] + product(shifted_next, act_next, step)
         half_full[step] = total
         half_sum[step] = total.astype(jnp.bfloat16)
         copies = []
@@ -337,32 +352,42 @@
             total = total + lane_shift(product, *OFFSETS[tap])
         block_ref[...] = total
 
-    partial_sum(0)
-    partial_sum(1)
     back_far.wait_recv()
     to_x[...] = (
         back[rows_of(far), :].astype(jnp.float32) + from_sib[1].astype(jnp.float32)
     ).astype(jnp.bfloat16)
     back_x = remote(to_x, from_x, 5, far_id)
     back_x.start()
-    partial_sum(2)
-    sum_pair(0)
-    partial_sum(3)
-    partial_sum(4)
-    sum_pair(1)
-    partial_sum(5)
+    g_y.wait_recv()
+    for tap, (row_step, col_step) in enumerate(OFFSETS):
+        shifted_next[tap * local_ch : (tap + 1) * local_ch, :] = lane_shift(
+            g_next[...].astype(jnp.float32), -row_step, -col_step
+        ).astype(jnp.bfloat16)
+    act_forward.wait_recv()
+    for step in range(CHUNKS):
+        own_sum(step)
+    next_far.wait_recv()
+    next_forward = remote(
+        act_next.at[rows_of(far)], act_next.at[rows_of(far)], extra + 4, sib_id
+    )
+    next_forward.start()
+    next_sib.wait_recv()
+    next_forward.wait_recv()
+    for step in range(CHUNKS):
+        sum_pair(step)
+        if step >= 4:
+            sum_line(step - 4)
     conv_taps(0, 3)
-    sum_line(0)
-    sum_pair(2)
+    share_pair(0)
+    sum_line(2)
     conv_taps(3, 6)
-    share_pair(0)
-    sum_line(1)
-    sum_pair(3)
-    conv_taps(6, 9)
     share_half(0)
     share_pair(1)
-    sum_line(2)
-    sum_pair(4)
+    sum_line(3)
+    conv_taps(6, 9)
+    share_half(1)
+    share_pair(2)
+    sum_line(4)
 
     back_own.wait_recv()
     back_x.wait_recv()
@@ -376,31 +401,27 @@
         pre_act, normed = pre_ref[rows, :], normed_ref[rows, :]
         sigmoid_val = jax.nn.sigmoid(pre_act)
         grad_pre = grad_act * sigmoid_val * (1.0 + pre_act * (1.0 - sigmoid_val))
-        grad_norm = grad_pre * gain_ref[rows, :]
+        grad_norm = grad_pre * affine_ref[rows, 0:1]
         mean_first = jnp.sum(grad_norm) * count
         mean_second = jnp.sum(grad_norm * normed) * count
         igrad_ref[rows, :] = g_ref[rows, :] + inv_devs[group] * (
             grad_norm - mean_first - normed * mean_second
         )
 
-    share_half(1)
-    share_pair(2)
-    sum_line(3)
-    sum_pair(5)
     share_half(2)
     share_pair(3)
-    sum_line(4)
+    sum_line(5)
     share_half(3)
     share_pair(4)
-    sum_line(5)
     share_half(4)
     share_pair(5)
     share_half(5)
     for copy in yg_copies:
         copy.wait_recv()
-    for copy in [act_sib, act_far, act_forward, back_far, back_own, back_x]:
+    singles = [act_sib, act_far, act_forward, back_far, back_own, back_x]
+    for copy in singles + [act_y, g_y, next_far, next_sib, next_forward]:
         copy.wait_send()
-    for copies in z_copies + [skip_copies, next_copies, y_copies, yg_copies]:
+    for copies in z_copies + [skip_copies, next_copies, yg_copies]:
         for copy in copies:
             copy.wait_send()
 
@@ -423,8 +444,9 @@
     all_rows = (taps * local_ch + unit - 1) // unit * unit
     half = all_rows // CHUNKS // DP_Y
     shard = half // DP_Z
-    copies = 6 + 8 * CHUNKS
+    copies = 6 + 8 * CHUNKS + 5
     vmem = pl.BlockSpec(memory_space=pltpu.VMEM)
+    hbm = pl.BlockSpec(memory_space=pltpu.HBM)
     flops = 2 * 3 * taps * local_ch * channels * width
     block_out, input_grad, summed = pl.pallas_call(
         step_kernel,
@@ -433,12 +455,18 @@
             jax.ShapeDtypeStruct(inputs.shape, jnp.float32),
             jax.ShapeDtypeStruct((all_rows, channels), jnp.bfloat16),
         ),
-        in_specs=[vmem, vmem, vmem, pl.BlockSpec(memory_space=pl.ANY), vmem],
+        in_specs=[hbm, vmem, hbm, hbm],
         out_specs=(vmem, vmem, vmem),
         scratch_shapes=[
+            pltpu.VMEM((local_ch, width), jnp.float32),
+            pltpu.VMEM((local_ch, width), jnp.float32),
             pltpu.VMEM((taps * local_ch, channels), jnp.float32),
             pltpu.VMEM((taps * local_ch, channels), jnp.bfloat16),
             pltpu.VMEM((channels, width), jnp.bfloat16),
+            pltpu.VMEM((channels, width), jnp.bfloat16),
+            pltpu.VMEM((local_ch, width), jnp.bfloat16),
+            pltpu.VMEM((local_ch, width), jnp.bfloat16),
+            pltpu.VMEM((all_rows, width), jnp.bfloat16),
             pltpu.VMEM((all_rows, width), jnp.bfloat16),
             pltpu.VMEM((local_ch, width), jnp.float32),
             pltpu.VMEM((local_ch, width), jnp.float32),
@@ -446,13 +474,10 @@
             pltpu.VMEM((2, local_ch, width), jnp.bfloat16),
             pltpu.VMEM((local_ch, width), jnp.bfloat16),
             pltpu.VMEM((local_ch, width), jnp.bfloat16),
-            pltpu.VMEM((all_rows, channels), jnp.float32),
-            pltpu.VMEM((all_rows, channels), jnp.bfloat16),
-            pltpu.VMEM((CHUNKS, half, channels), jnp.bfloat16),
             pltpu.VMEM((CHUNKS, half, channels), jnp.float32),
             pltpu.VMEM((CHUNKS, half, channels), jnp.bfloat16),
             pltpu.VMEM((CHUNKS, DP_Z - 1, shard, channels), jnp.bfloat16),
-            pltpu.SemaphoreType.DMA,
+            pltpu.SemaphoreType.DMA((3,)),
             pltpu.SemaphoreType.DMA((copies,)),
             pltpu.SemaphoreType.DMA((copies,)),
         ],
@@ -464,8 +489,7 @@
         ),
     )(
         inputs,
-        norm_gain[:, None],
-        norm_bias[:, None],
+        jnp.stack([norm_gain, norm_bias], axis=1),
         conv_weight.reshape(taps * local_ch, channels),
         out_grad,
     )

time: 82 us -> 92.6 us (1.13)
  Pallas kernels: 73.6 us -> 84.9 us
  local copies, waits for them, and re-layouts: 7.46 us -> 6 us
    pallas_call x1, Pallas kernels: 67.4 us -> 78.7 us  [fused_body(): pl.pallas_call(step_kernel, out_shape=(jax.ShapeDtypeStruct(inputs.shape,...]
    broadcast_in_dim x2 -> x0, local copies, waits for them, and re-layouts: 1.57 us -> none  [the longest x1 0.79 us: fused_body(): norm_bias[:, None]]
where the time goes in v2:
time: 92.6 us; the launch traced here: 92.3 us
  Pallas kernels  84.9 us (92%)
  local copies, waits for them, and re-layouts  6 us (6%)
    pallas_call x1, Pallas kernels, fused_body(): pl.pallas_call(step_kernel, out_shape=(jax.ShapeDtypeStruct(inputs.shape,...  78.7 us
    pallas_call x1, Pallas kernels, fused_body(): pl.pallas_call(functools.partial(adam_kernel, scale), grid=(taps,), out_s...  6.2 us
    unnamed x12, local copies, waits for them, and re-layouts  5.9 us

profile of v2, /device:TPU:0, one launch (start us, length us, event | category | flops | bytes accessed | tf_op | source)
XLA Modules:
  0.0 92.3 jit_solution(3843352544110513508)
XLA Ops:
  0.6 0.7 pad_maximum_fusion
  1.3 0.1 copy.14.affine_ref
  1.5 0.0 copy-start
  1.5 2.0 %copy-done = f32[9,160,640]{2,1,0:T(8,128)S(1)} copy-done((f32[9,160,640]{2,1,0:T(8,128)S(1)}, f32[9,160,640]{2,1,0:T(8,128)}, u32[]{:S(2)}) %copy-start) | copy-done | bytes 3686424
  3.5 0.0 copy-start.3
  3.5 1.1 %copy-done.3 = f32[160,1024]{1,0:T(8,128)S(1)} copy-done((f32[160,1024]{1,0:T(8,128)S(1)}, f32[160,1024]{1,0:T(8,128)}, u32[]{:S(2)}) %copy-start.3) | copy-done | bytes 655384
  4.6 0.0 copy-start.4
  4.6 1.1 %copy-done.4 = f32[160,1024]{1,0:T(8,128)S(1)} copy-done((f32[160,1024]{1,0:T(8,128)S(1)}, f32[160,1024]{1,0:T(8,128)}, u32[]{:S(2)}) %copy-start.4) | copy-done | bytes 655384
  5.7 0.0 copy-start.1
  5.7 0.0 copy-start.2
  5.7 78.7 %shard_map.110 = (f32[160,1024]{1,0:T(8,128)S(1)}, f32[160,1024]{1,0:T(8,128)S(1)}, bf16[1536,640]{1,0:T(8,128)(2,1)S(1)}) custom-call(f32[160,1024]{1,0:T(8,128)S(1)} %copy-done.3, f32[160,2]{1,0:T(8,128)S(1)} %copy.14.affine_ref, f32[1440,640]{1,0:T(8,128)S(1)} %bitcast.8, f32[160,1024]{1,0:T(8,128)S(1)} %copy-done.4), custom_call_target="tpu_custom_call" | custom-call | flops 5662310400 | bytes 8000000 | tf_op jit(solution)/shard_map/pallas_call | solution.py:451
  84.4 0.0 copy-done.1
  84.4 0.0 copy-done.2
  84.4 6.2 %shard_map.111 = (f32[1440,640]{1,0:T(8,128)}, f32[1440,640]{1,0:T(8,128)}, f32[1440,640]{1,0:T(8,128)}) custom-call(bf16[1536,640]{1,0:T(8,128)(2,1)S(1)} %get-tuple-element.13.sum_ref, f32[1440,640]{1,0:T(8,128)S(1)} %bitcast.9, f32[1440,640]{1,0:T(8,128)S(1)} %bitcast.10, f32[1440,640]{1,0:T(8,128)S(1)} %bitcast.11), custom_call_target="tpu_custom_call" | custom-call | flops 14745600 | bytes 23961600 | tf_op jit(solution)/shard_map/pallas_call | solution.py:499
  90.6 0.8 copy.17
  91.5 0.8 copy.18
Async XLA Ops:
  1.5 2.0 %copy-start = (f32[9,160,640]{2,1,0:T(8,128)S(1)}, f32[9,160,640]{2,1,0:T(8,128)}, u32[]{:S(2)}) copy-start(f32[9,160,640]{2,1,0:T(8,128)} %param.10) | copy-start | bytes 11059204
  3.5 1.1 %copy-start.3 = (f32[160,1024]{1,0:T(8,128)S(1)}, f32[160,1024]{1,0:T(8,128)}, u32[]{:S(2)}) copy-start(f32[160,1024]{1,0:T(8,128)} %x_hbm.1) | copy-start | bytes 1966084
  4.6 1.1 %copy-start.4 = (f32[160,1024]{1,0:T(8,128)S(1)}, f32[160,1024]{1,0:T(8,128)}, u32[]{:S(2)}) copy-start(f32[160,1024]{1,0:T(8,128)} %g_hbm.1) | copy-start | bytes 1966084
  5.7 78.7 %copy-start.1 = (f32[9,160,640]{2,1,0:T(8,128)S(1)}, f32[9,160,640]{2,1,0:T(8,128)}, u32[]{:S(2)}) copy-start(f32[9,160,640]{2,1,0:T(8,128)} %param.11) | copy-start | bytes 11059204
  5.7 78.7 %copy-start.2 = (f32[9,160,640]{2,1,0:T(8,128)S(1)}, f32[9,160,640]{2,1,0:T(8,128)}, u32[]{:S(2)}) copy-start(f32[9,160,640]{2,1,0:T(8,128)} %param.12) | copy-start | bytes 11059204

commit v3 on v1

--- a/solution.py
+++ b/solution.py
@@ -229,26 +229,19 @@
     spare = all_rows - taps * local_ch
     shifted_g[taps * local_ch :, :] = jnp.zeros((spare, width), jnp.bfloat16)
 
-    w_copy.wait()
-    w_half[...] = w_full[...].astype(jnp.bfloat16)
-
     tile = 512
 
-    def back_tile(step, carry):
-        columns = pl.ds(pl.multiple_of(step * tile, tile), tile)
+    def back_tile(step):
+        columns = slice(step * tile, (step + 1) * tile)
         back[:, columns] = lax.dot_general(
             w_half[...],
             shifted_g[: taps * local_ch, columns],
             (((0,), (0,)), ((), ())),
             preferred_element_type=jnp.float32,
         ).astype(jnp.bfloat16)
-        return carry
-
-    lax.fori_loop(0, width // tile, back_tile, 0)
+
     back_far = remote(back.at[rows_of(far_sib)], from_sib.at[1], 4, sib_id)
     back_own = remote(back.at[rows_of(sib)], from_sib.at[0], 3, sib_id)
-    back_far.start()
-    back_own.start()
 
     act_far.wait_recv()
     act_forward = remote(act.at[rows_of(far)], act.at[rows_of(far)], 2, sib_id)
@@ -261,8 +254,8 @@
     def half_rows(step, index):
         return pl.ds(pl.multiple_of(step * chunk + index * half, half), half)
 
-    def partial_sum(step):
-        rows = slice(step * chunk, (step + 1) * chunk)
+    def partial_sums(first, last):
+        rows = slice(first * chunk, last * chunk)
         product = lax.dot_general(
             shifted_g[rows, :],
             act[...],
@@ -271,9 +264,11 @@
         )
         own_full[rows, :] = product
         part[rows, :] = product.astype(jnp.bfloat16)
-        copy = remote(part.at[half_rows(step, 1 - pos_y)], from_y.at[step], 6 + 8 * step, y_id)
-        copy.start()
-        y_copies.append(copy)
+        for step in range(first, last):
+            sent = part.at[half_rows(step, 1 - pos_y)]
+            copy = remote(sent, from_y.at[step], 6 + 8 * step, y_id)
+            copy.start()
+            y_copies.append(copy)
 
     def place(index_z):
         return index_z % 2 * 2 + index_z // 2
@@ -328,41 +323,52 @@
 
     def conv_taps(first, last):
         total = x_ref[...] if first == 0 else block_ref[...]
+        product = jnp.dot(
+            w_half[first * local_ch : last * local_ch, :],
+            act[...],
+            preferred_element_type=jnp.float32,
+        )
         for tap in range(first, last):
-            product = jnp.dot(
-                w_half[tap * local_ch : (tap + 1) * local_ch, :],
-                act[...],
-                preferred_element_type=jnp.float32,
-            )
-            total = total + lane_shift(product, *OFFSETS[tap])
+            rows = slice((tap - first) * local_ch, (tap - first + 1) * local_ch)
+            total = total + lane_shift(product[rows], *OFFSETS[tap])
         block_ref[...] = total
 
-    partial_sum(0)
-    partial_sum(1)
+    partial_sums(0, 2)
+    partial_sums(2, 4)
+    sum_pair(0)
+    partial_sums(4, 6)
+    sum_pair(1)
+    w_copy.wait()
+    w_half[...] = w_full[...].astype(jnp.bfloat16)
+    back_tile(0)
+    sum_pair(2)
+    sum_line(0)
+    back_tile(1)
+    back_far.start()
+    back_own.start()
+    sum_pair(3)
+    sum_line(1)
+    share_pair(0)
+    conv_taps(0, 3)
+    sum_pair(4)
+    sum_line(2)
+    share_pair(1)
+    share_half(0)
     back_far.wait_recv()
     to_x[...] = (
         back[rows_of(far), :].astype(jnp.float32) + from_sib[1].astype(jnp.float32)
     ).astype(jnp.bfloat16)
     back_x = remote(to_x, from_x, 5, far_id)
     back_x.start()
-    partial_sum(2)
-    sum_pair(0)
-    partial_sum(3)
-    partial_sum(4)
-    sum_pair(1)
-    partial_sum(5)
-    conv_taps(0, 3)
-    sum_line(0)
-    sum_pair(2)
     conv_taps(3, 6)
-    share_pair(0)
-    sum_line(1)
-    sum_pair(3)
+    sum_pair(5)
+    sum_line(3)
+    share_pair(2)
+    share_half(1)
     conv_taps(6, 9)
-    share_half(0)
-    share_pair(1)
-    sum_line(2)
-    sum_pair(4)
+    sum_line(4)
+    share_pair(3)
+    share_half(2)
 
     back_own.wait_recv()
     back_x.wait_recv()
@@ -383,18 +389,11 @@
             grad_norm - mean_first - normed * mean_second
         )
 
-    share_half(1)
-    share_pair(2)
-    sum_line(3)
-    sum_pair(5)
-    share_half(2)
-    share_pair(3)
-    sum_line(4)
+    sum_line(5)
+    share_pair(4)
     share_half(3)
-    share_pair(4)
-    sum_line(5)
+    share_pair(5)
     share_half(4)
-    share_pair(5)
     share_half(5)
     for copy in yg_copies:
         copy.wait_recv()

time: 82 us -> 82 us (level)
  no operation moved by 1% of the time
where the time goes in v3:
time: 82 us; the launch traced here: 81.7 us
  Pallas kernels  73.6 us (90%)
  local copies, waits for them, and re-layouts  7.46 us (9%)
    pallas_call x1, Pallas kernels, fused_body(): pl.pallas_call(step_kernel, out_shape=(jax.ShapeDtypeStruct(inputs.shape,...  67.4 us
    pallas_call x1, Pallas kernels, fused_body(): pl.pallas_call(functools.partial(adam_kernel, scale), grid=(taps,), out_s...  6.2 us
    unnamed x12, local copies, waits for them, and re-layouts  5.89 us

profile of v3, /device:TPU:0, one launch (start us, length us, event | category | flops | bytes accessed | tf_op | source)
XLA Modules:
  0.0 81.7 jit_solution(7538235636746514141)
XLA Ops:
  0.6 0.8 copy.12.gain_ref
  1.4 0.8 copy.13.bias_ref
  2.2 0.0 copy-start
  2.2 2.0 %copy-done = f32[9,160,640]{2,1,0:T(8,128)S(1)} copy-done((f32[9,160,640]{2,1,0:T(8,128)S(1)}, f32[9,160,640]{2,1,0:T(8,128)}, u32[]{:S(2)}) %copy-start) | copy-done | bytes 3686424
  4.3 0.0 copy-start.3
  4.3 1.1 %copy-done.3 = f32[160,1024]{1,0:T(8,128)S(1)} copy-done((f32[160,1024]{1,0:T(8,128)S(1)}, f32[160,1024]{1,0:T(8,128)}, u32[]{:S(2)}) %copy-start.3) | copy-done | bytes 655384
  5.3 0.0 copy-start.4
  5.4 1.1 %copy-done.4 = f32[160,1024]{1,0:T(8,128)S(1)} copy-done((f32[160,1024]{1,0:T(8,128)S(1)}, f32[160,1024]{1,0:T(8,128)}, u32[]{:S(2)}) %copy-start.4) | copy-done | bytes 655384
  6.4 0.0 copy-start.1
  6.4 0.0 copy-start.2
  6.4 67.4 %shard_map.110 = (f32[160,1024]{1,0:T(8,128)S(1)}, f32[160,1024]{1,0:T(8,128)S(1)}, bf16[1536,640]{1,0:T(8,128)(2,1)S(1)}) custom-call(f32[160,1024]{1,0:T(8,128)S(1)} %copy-done.3, f32[160,1]{1,0:T(8,128)S(1)} %copy.12.gain_ref, f32[160,1]{1,0:T(8,128)S(1)} %copy.13.bias_ref, f32[1440,640]{1,0:T(8,128)S(1)} %bitcast.8, f32[160,1024]{1,0:T(8,128)S(1)} %copy-done.4), custom_call_target="tpu_custom_call" | custom-call | flops 5662310400 | bytes 8000000 | tf_op jit(solution)/shard_map/pallas_call | solution.py:428
  73.8 0.0 copy-done.1
  73.8 0.0 copy-done.2
  73.8 6.2 %shard_map.111 = (f32[1440,640]{1,0:T(8,128)}, f32[1440,640]{1,0:T(8,128)}, f32[1440,640]{1,0:T(8,128)}) custom-call(bf16[1536,640]{1,0:T(8,128)(2,1)S(1)} %get-tuple-element.13.sum_ref, f32[1440,640]{1,0:T(8,128)S(1)} %bitcast.9, f32[1440,640]{1,0:T(8,128)S(1)} %bitcast.10, f32[1440,640]{1,0:T(8,128)S(1)} %bitcast.11), custom_call_target="tpu_custom_call" | custom-call | flops 14745600 | bytes 23961600 | tf_op jit(solution)/shard_map/pallas_call | solution.py:474
  80.1 0.8 %copy.16 = f32[160,1024]{1,0:T(8,128)} copy(f32[160,1024]{1,0:T(8,128)S(1)} %get-tuple-element.22) | data formatting | bytes 1310720
  80.9 0.8 %copy.17 = f32[160,1024]{1,0:T(8,128)} copy(f32[160,1024]{1,0:T(8,128)S(1)} %get-tuple-element.23) | data formatting | bytes 1310720
Async XLA Ops:
  2.2 2.0 %copy-start = (f32[9,160,640]{2,1,0:T(8,128)S(1)}, f32[9,160,640]{2,1,0:T(8,128)}, u32[]{:S(2)}) copy-start(f32[9,160,640]{2,1,0:T(8,128)} %param.10) | copy-start | bytes 11059204
  4.3 1.1 %copy-start.3 = (f32[160,1024]{1,0:T(8,128)S(1)}, f32[160,1024]{1,0:T(8,128)}, u32[]{:S(2)}) copy-start(f32[160,1024]{1,0:T(8,128)} %x_ref.1) | copy-start | bytes 1966084
  5.3 1.1 %copy-start.4 = (f32[160,1024]{1,0:T(8,128)S(1)}, f32[160,1024]{1,0:T(8,128)}, u32[]{:S(2)}) copy-start(f32[160,1024]{1,0:T(8,128)} %g_ref.1) | copy-start | bytes 1966084
  6.4 67.4 %copy-start.1 = (f32[9,160,640]{2,1,0:T(8,128)S(1)}, f32[9,160,640]{2,1,0:T(8,128)}, u32[]{:S(2)}) copy-start(f32[9,160,640]{2,1,0:T(8,128)} %param.11) | copy-start | bytes 11059204
  6.4 67.4 %copy-start.2 = (f32[9,160,640]{2,1,0:T(8,128)S(1)}, f32[9,160,640]{2,1,0:T(8,128)}, u32[]{:S(2)}) copy-start(f32[9,160,640]{2,1,0:T(8,128)} %param.12) | copy-start | bytes 11059204
